TPU v7x, 32 devices: a whole 2x2x4 slice. The times are simulated.
32 devices in a mesh: sub: 16 (over z, y, x), rhs: 2 (over core).
Axes of the slice: x: 2, y: 2, z: 4, core: 2. Of those that a mesh axis runs over, the one named last changes fastest.
Arguments:
- schur_block: bfloat16 [32, 1024, 1024], P('sub', 'rhs'), may hold values from -1 to 4, as said below
- scaling: float32 [32, 1024], P('sub'), may hold values from 0.25 to 1.75
- gravity_load: float32 [32, 1024, 256], P('sub', None, 'rhs'), may hold values from -100 to 100
- pressure: bfloat16 [1024, 4, 256], P('sub', None, 'rhs'), may hold values from -6 to 6
- block_target: int32 [1024, 1], P('sub'), may hold values from 0 to 31; in each aligned block of 64 rows (0 to 63, 64 to 127, ...) at most 4 rows name the same one
- aero_interp: float32 [4, 1024], replicated, may hold values from -0.5 to 0.5
- partner_slot: int32 [4, 32], P(None, 'sub'), may hold values from 0 to 1, as said below
- corner_row: int32 [32, 8], P('sub'), may hold values from 0 to 1023
- corner_coarse: int32 [32, 8], P('sub'), may hold values from 0 to 127
- coarse_inverse: float32 [128, 128], P('sub'), may hold values from -1 to 6, as said below
Outputs:
- solution: float32 [32, 1024, 256], P('sub', None, 'rhs')
Inputs may be any that keep to these rules, and one draw needn't show every extreme that they name: `block_target`: at most 4 of the blocks of one device name the same subdomain; in some device's blocks one subdomain is named exactly 4 times; every subdomain is named by some block. In round k, subdomain s on device d = s // 2 is paired with subdomain (d xor 2^k) * 2 + partner_slot[k, s]; the pairing is mutual. `schur_block`: each matrix is symmetric. `coarse_inverse`: symmetric.
All inputs are finite; a program needn't handle non-finite values.
Results may differ from a plain program's by a relative error of at most 0.0027.
Values may be sent and summed in bfloat16 or wider, within the bound.
A program may use at most 64 MiB of HBM per device.

v0:
```python
import jax
import jax.numpy as jnp
from jax import lax
from jax.sharding import PartitionSpec as P

SUB_DEV = 2
FACES = 4
MOST = 4
ITERS = 2
FW = 256
coupling = 2.0


def swapped(shard, axis, distance):
    return lax.ppermute(shard, axis, [(i, i ^ 1 << distance) for i in range(lax.axis_size(axis))])


def all_sum(value):
    distance = 0
    while 1 << distance < lax.axis_size("sub"):
        value = value + swapped(value, "sub", distance)
        distance += 1
    return value


def schur_apply(schur_block, rounded):
    half_rows = jnp.einsum(
        "snm,smc->snc",
        schur_block,
        lax.all_gather(rounded, "rhs", axis=2, tiled=True),
        preferred_element_type=jnp.float32,
    )
    return lax.all_to_all(half_rows, "rhs", split_axis=2, concat_axis=1, tiled=True)


def jump_terms(rounded, partner_slot):
    face_terms = []
    for face_index in range(FACES):
        own_face = rounded[:, face_index * FW : (face_index + 1) * FW, :]
        partner_face = swapped(own_face, "sub", face_index)
        select = (
            partner_slot[face_index][:, None] == jnp.arange(SUB_DEV, dtype=jnp.int32)[None, :]
        ).astype(jnp.bfloat16)
        picked = jnp.einsum("sj,jfc->sfc", select, partner_face, preferred_element_type=jnp.float32)
        face_terms.append(coupling * (own_face.astype(jnp.float32) - picked))
    return jnp.concatenate(face_terms, axis=1)


def operator(direction, schur_block, partner_slot):
    rounded = direction.astype(jnp.bfloat16)
    return schur_apply(schur_block, rounded) + jump_terms(rounded, partner_slot)


def coarse_solve(coarse, coarse_inverse):
    own_rows = jnp.dot(coarse_inverse, coarse, precision=lax.Precision.HIGHEST)
    start = lax.axis_index("sub") * own_rows.shape[0]
    whole = jnp.zeros_like(coarse)
    return all_sum(lax.dynamic_update_slice(whole, own_rows, (start, 0)))


def add_corners(solved, corner_row, corner_coarse, residual):
    sub_rows = jnp.arange(SUB_DEV, dtype=jnp.int32)[:, None]
    return jnp.zeros_like(residual).at[sub_rows, corner_row].add(solved[corner_coarse])


def precondition(residual, schur_block, scaling, corner_row, corner_coarse, coarse_inverse):
    columns = residual.shape[2]
    weight_col = scaling[:, :, None]
    dirichlet = weight_col * schur_apply(schur_block, (weight_col * residual).astype(jnp.bfloat16))
    sub_rows = jnp.arange(SUB_DEV, dtype=jnp.int32)[:, None]
    picked = residual[sub_rows, corner_row]
    partial_sum = (
        jnp.zeros((coarse_inverse.shape[1], columns), jnp.float32)
        .at[corner_coarse.reshape(-1)]
        .add(picked.reshape(-1, columns))
    )
    coarse = all_sum(partial_sum)
    solved = coarse_solve(coarse, coarse_inverse)
    precond = dirichlet + add_corners(solved, corner_row, corner_coarse, residual)
    product_value = all_sum(jnp.sum(residual * precond, axis=(0, 1)))
    return (precond, product_value)


def on_device(
    schur_block,
    scaling,
    gravity_load,
    pressure,
    block_target,
    aero_interp,
    partner_slot,
    corner_row,
    corner_coarse,
    coarse_inverse,
):
    sub_count = lax.axis_size("sub")
    all_subdomains = SUB_DEV * sub_count
    columns = gravity_load.shape[2]
    points = pressure.shape[1]
    target = block_target[:, 0]
    matches = target[:, None] == target[None, :]
    before = jnp.tril(matches, -1)
    rank_in = jnp.sum(before, axis=1, dtype=jnp.int32)
    slot_index = target * MOST + rank_in
    buffer = (
        jnp.zeros((all_subdomains * MOST, points, columns), jnp.bfloat16)
        .at[slot_index]
        .set(pressure)
    )
    arrived = lax.all_to_all(buffer, "sub", split_axis=0, concat_axis=0, tiled=True)
    load_sum = jnp.sum(
        arrived.reshape(sub_count, SUB_DEV, MOST, points, columns), axis=(0, 2), dtype=jnp.float32
    )
    force_total = gravity_load + jnp.einsum(
        "pm,spc->smc", aero_interp, load_sum, precision=lax.Precision.HIGHEST
    )
    solution = jnp.zeros_like(force_total)
    residual = force_total
    precond, precond_dot = precondition(
        residual, schur_block, scaling, corner_row, corner_coarse, coarse_inverse
    )
    direction = precond
    for step_index in range(ITERS):
        applied = operator(direction, schur_block, partner_slot)
        curvature = all_sum(jnp.sum(direction * applied, axis=(0, 1)))
        step_size = precond_dot / curvature
        solution = solution + step_size * direction
        residual = residual - step_size * applied
        if step_index + 1 < ITERS:
            precond, next_product = precondition(
                residual, schur_block, scaling, corner_row, corner_coarse, coarse_inverse
            )
            direction = precond + next_product / precond_dot * direction
            precond_dot = next_product
    return solution


def solution(mesh):
    return jax.shard_map(
        on_device,
        mesh=mesh,
        in_specs=(
            P("sub", "rhs", None),
            P("sub", None),
            P("sub", None, "rhs"),
            P("sub", None, "rhs"),
            P("sub", None),
            P(),
            P(None, "sub"),
            P("sub", None),
            P("sub", None),
            P("sub", None),
        ),
        out_specs=P("sub", None, "rhs"),
        check_vma=False,
    )
```

profile of v0, /device:TPU:0, one launch (start us, length us, event | category | flops | bytes accessed | tf_op | source)
XLA Modules:
  0.0 293.3 jit_solution(6070715701411228412)
XLA Ops:
  8.9 6.8 %scatter_fusion = bf16[128,4,128]{2,1,0:T(4,128)(2,1)} fusion(bf16[128,4,128]{2,1,0:T(4,128)(2,1)} %broadcast_in_dim.12, s32[64]{0:T(128)S(1)} %fusion.24, bf16[64,4,128]{2,1,0:T(4,128)(2,1)} %param.13), kind=kCustom, calls=%fused_computation.4 | custom fusion | bytes 196864 | tf_op jit(solution)/shard_map/scatter | solution.py:108
  15.7 8.4 %all-to-all-start = ((bf16[128,4,128]{2,1,0:T(4,128)(2,1)}), bf16[128,4,128]{2,1,0:T(4,128)(2,1)S(1)}, u32[]{:S(2)}, u32[]{:S(2)}) async-start(bf16[128,4,128]{2,1,0:T(4,128)(2,1)} %scatter_fusion), calls=%async_computation | async-start | bytes 262144 | tf_op jit(solution)/shard_map/all_to_all | solution.py:110
  24.8 2.5 copy.107
  27.5 4.4 %all-to-all-done = bf16[128,4,128]{2,1,0:T(4,128)(2,1)S(1)} async-done(((bf16[128,4,128]{2,1,0:T(4,128)(2,1)}), bf16[128,4,128]{2,1,0:T(4,128)(2,1)S(1)}, u32[]{:S(2)}, u32[]{:S(2)}) %all-to-all-start) | async-done | bytes 131104 | tf_op jit(solution)/shard_map/all_to_all | solution.py:110
  31.9 3.1 %multiply_convert_fusion.1 = (bf16[2,1024,128]{1,2,0:T(8,128)(2,1)}, f32[2,1024,128]{1,2,0:T(8,128)S(1)}) fusion(f32[2,1024]{1,0:T(2,128)S(1)} %copy-done.9, f32[2,1024,128]{1,2,0:T(8,128)} %copy.107, f32[2,4,128]{2,1,0:T(4,128)S(1)} %convert_reduce_fusion, f32[4,1024]{1,0:T(4,128)S(1)} %copy-done.12), kind=kOutput, calls=%fused_computation.32 | convolution fusion | flops 13369344 | bytes 2650112 | tf_op jit(solution)/shard_map/pm,spc->smc/dot_general | solution.py:114
  39.0 3.2 %collective-permute-done = f32[128,128]{1,0:T(8,128)S(1)} collective-permute-done((f32[128,128]{1,0:T(8,128)S(1)}, f32[128,128]{1,0:T(8,128)S(1)}, u32[]{:S(2)}, u32[]{:S(2)}) %collective-permute-start) | collective-permute-done | bytes 65568 | tf_op jit(solution)/shard_map/ppermute | solution.py:15
  43.0 3.5 %collective-permute-done.1 = f32[128,128]{1,0:T(8,128)S(1)} collective-permute-done((f32[128,128]{1,0:T(8,128)S(1)}, f32[128,128]{1,0:T(8,128)S(1)}, u32[]{:S(2)}, u32[]{:S(2)}) %collective-permute-start.1) | collective-permute-done | bytes 65568 | tf_op jit(solution)/shard_map/ppermute | solution.py:15
  47.4 3.8 %collective-permute-done.2 = f32[128,128]{1,0:T(8,128)S(1)} collective-permute-done((f32[128,128]{1,0:T(8,128)S(1)}, f32[128,128]{1,0:T(8,128)S(1)}, u32[]{:S(2)}, u32[]{:S(2)}) %collective-permute-start.2) | collective-permute-done | bytes 65568 | tf_op jit(solution)/shard_map/ppermute | solution.py:15
  52.0 5.0 %collective-permute-done.3 = f32[128,128]{1,0:T(8,128)S(1)} collective-permute-done((f32[128,128]{1,0:T(8,128)S(1)}, f32[128,128]{1,0:T(8,128)S(1)}, u32[]{:S(2)}, u32[]{:S(2)}) %collective-permute-start.3) | collective-permute-done | bytes 65568 | tf_op jit(solution)/shard_map/ppermute | solution.py:15
  58.0 3.4 %collective-permute-done.4 = f32[128,128]{1,0:T(8,128)S(1)} collective-permute-done((f32[128,128]{1,0:T(8,128)S(1)}, f32[128,128]{1,0:T(8,128)S(1)}, u32[]{:S(2)}, u32[]{:S(2)}) %collective-permute-start.4) | collective-permute-done | bytes 65568 | tf_op jit(solution)/shard_map/ppermute | solution.py:15
  62.2 3.5 %collective-permute-done.5 = f32[128,128]{1,0:T(8,128)S(1)} collective-permute-done((f32[128,128]{1,0:T(8,128)S(1)}, f32[128,128]{1,0:T(8,128)S(1)}, u32[]{:S(2)}, u32[]{:S(2)}) %collective-permute-start.5) | collective-permute-done | bytes 65568 | tf_op jit(solution)/shard_map/ppermute | solution.py:15
  66.0 4.1 %collective-permute-done.6 = f32[128,128]{1,0:T(8,128)S(1)} collective-permute-done((f32[128,128]{1,0:T(8,128)S(1)}, f32[128,128]{1,0:T(8,128)S(1)}, u32[]{:S(2)}, u32[]{:S(2)}) %collective-permute-start.6) | collective-permute-done | bytes 65568 | tf_op jit(solution)/shard_map/ppermute | solution.py:15
  70.4 5.1 %collective-permute-done.7 = f32[128,128]{1,0:T(8,128)S(1)} collective-permute-done((f32[128,128]{1,0:T(8,128)S(1)}, f32[128,128]{1,0:T(8,128)S(1)}, u32[]{:S(2)}, u32[]{:S(2)}) %collective-permute-start.7) | collective-permute-done | bytes 65568 | tf_op jit(solution)/shard_map/ppermute | solution.py:15
  78.9 4.6 %all_to_all.77 = f32[2,512,256]{1,0,2:T(2,128)S(1)} all-to-all(f32[2,512,256]{1,0,2:T(2,128)S(1)} %copy.108), channel_id=1, replica_groups=mesh['sub'=16,'rhs'=2] {'rhs'}, dimensions={2} | all-to-all | bytes 2097152 | tf_op jit(solution)/shard_map/all_to_all | solution.py:33
  119.4 4.6 %all_to_all.78 = f32[2,512,256]{1,0,2:T(2,128)S(1)} all-to-all(f32[2,512,256]{1,0,2:T(2,128)S(1)} %copy.114), channel_id=1, replica_groups=mesh['sub'=16,'rhs'=2] {'rhs'}, dimensions={2} | all-to-all | bytes 2097152 | tf_op jit(solution)/shard_map/all_to_all | solution.py:33
  125.8 3.1 %all_to_all.63 = f32[2,1024,128]{1,2,0:T(8,128)} reshape(f32[2,2,512,128]{2,1,3,0:T(2,128)} %bitcast.106) | data formatting | bytes 2097152 | tf_op jit(solution)/shard_map/all_to_all | solution.py:33
  149.2 2.5 copy.128
  154.6 3.1 %collective-permute-done.20 = f32[128,128]{1,0:T(8,128)S(1)} collective-permute-done((f32[128,128]{1,0:T(8,128)S(1)}, f32[128,128]{1,0:T(8,128)S(1)}, u32[]{:S(2)}, u32[]{:S(2)}) %collective-permute-start.20) | collective-permute-done | bytes 65568 | tf_op jit(solution)/shard_map/ppermute | solution.py:15
  158.9 3.1 %collective-permute-done.21 = f32[128,128]{1,0:T(8,128)S(1)} collective-permute-done((f32[128,128]{1,0:T(8,128)S(1)}, f32[128,128]{1,0:T(8,128)S(1)}, u32[]{:S(2)}, u32[]{:S(2)}) %collective-permute-start.21) | collective-permute-done | bytes 65568 | tf_op jit(solution)/shard_map/ppermute | solution.py:15
  163.5 2.8 collective-permute-done.22
  168.5 3.1 %collective-permute-done.23 = f32[128,128]{1,0:T(8,128)S(1)} collective-permute-done((f32[128,128]{1,0:T(8,128)S(1)}, f32[128,128]{1,0:T(8,128)S(1)}, u32[]{:S(2)}, u32[]{:S(2)}) %collective-permute-start.23) | collective-permute-done | bytes 65568 | tf_op jit(solution)/shard_map/ppermute | solution.py:15
  173.0 3.1 %collective-permute-done.24 = f32[128,128]{1,0:T(8,128)S(1)} collective-permute-done((f32[128,128]{1,0:T(8,128)S(1)}, f32[128,128]{1,0:T(8,128)S(1)}, u32[]{:S(2)}, u32[]{:S(2)}) %collective-permute-start.24) | collective-permute-done | bytes 65568 | tf_op jit(solution)/shard_map/ppermute | solution.py:15
  177.2 3.1 %collective-permute-done.25 = f32[128,128]{1,0:T(8,128)S(1)} collective-permute-done((f32[128,128]{1,0:T(8,128)S(1)}, f32[128,128]{1,0:T(8,128)S(1)}, u32[]{:S(2)}, u32[]{:S(2)}) %collective-permute-start.25) | collective-permute-done | bytes 65568 | tf_op jit(solution)/shard_map/ppermute | solution.py:15
  181.8 2.8 collective-permute-done.26
  186.8 3.1 %collective-permute-done.27 = f32[128,128]{1,0:T(8,128)S(1)} collective-permute-done((f32[128,128]{1,0:T(8,128)S(1)}, f32[128,128]{1,0:T(8,128)S(1)}, u32[]{:S(2)}, u32[]{:S(2)}) %collective-permute-start.27) | collective-permute-done | bytes 65568 | tf_op jit(solution)/shard_map/ppermute | solution.py:15
  193.4 4.6 %all_to_all.79 = f32[2,512,256]{1,0,2:T(2,128)S(1)} all-to-all(f32[2,512,256]{1,0,2:T(2,128)S(1)} %copy.126), channel_id=1, replica_groups=mesh['sub'=16,'rhs'=2] {'rhs'}, dimensions={2} | all-to-all | bytes 2097152 | tf_op jit(solution)/shard_map/all_to_all | solution.py:33
  199.8 3.1 %all_to_all.67 = f32[2,1024,128]{1,2,0:T(8,128)} reshape(f32[2,2,512,128]{2,1,3,0:T(2,128)} %bitcast.108) | data formatting | bytes 2097152 | tf_op jit(solution)/shard_map/all_to_all | solution.py:33
  205.3 2.5 copy.129
  210.0 2.6 copy.130
  256.2 4.6 %all_to_all.80 = f32[2,512,256]{1,0,2:T(2,128)S(1)} all-to-all(f32[2,512,256]{1,0,2:T(2,128)S(1)} %copy.133), channel_id=1, replica_groups=mesh['sub'=16,'rhs'=2] {'rhs'}, dimensions={2} | all-to-all | bytes 2097152 | tf_op jit(solution)/shard_map/all_to_all | solution.py:33
  262.5 3.1 %all_to_all.71 = f32[2,1024,128]{1,2,0:T(8,128)} reshape(f32[2,2,512,128]{2,1,3,0:T(2,128)} %bitcast.110) | data formatting | bytes 2097152 | tf_op jit(solution)/shard_map/all_to_all | solution.py:33
  280.2 2.7 collective-permute-done.39
  (226 shorter events, 161.1 us)
Async XLA Ops:
  15.7 16.2 %all-to-all-start = ((bf16[128,4,128]{2,1,0:T(4,128)(2,1)}), bf16[128,4,128]{2,1,0:T(4,128)(2,1)S(1)}, u32[]{:S(2)}, u32[]{:S(2)}) async-start(bf16[128,4,128]{2,1,0:T(4,128)(2,1)} %scatter_fusion), calls=%async_computation | async-start | bytes 262144 | tf_op jit(solution)/shard_map/all_to_all | solution.py:110
  24.0 52.0 %all-gather.5.cloned.1.call-start = ((), (), s32[]{:S(2)}) async-start(), calls=%async_computation.5 | async-start | bytes 1572864 | tf_op jit(solution)/shard_map/all_gather | solution.py:30
  37.8 4.3 %collective-permute-start = (f32[128,128]{1,0:T(8,128)S(1)}, f32[128,128]{1,0:T(8,128)S(1)}, u32[]{:S(2)}, u32[]{:S(2)}) collective-permute-start(f32[128,128]{1,0:T(8,128)S(1)} %scatter_custom_fusion.1), channel_id=1, source_target_pairs={{0,2},{2,0},{4,6},{6,4},{8,10},{10,8},{12,14},{14,12},{16,18},{18,... | collective-permute-start | bytes 196616 | tf_op jit(solution)/shard_map/ppermute | solution.py:15
  42.2 4.3 %collective-permute-start.1 = (f32[128,128]{1,0:T(8,128)S(1)}, f32[128,128]{1,0:T(8,128)S(1)}, u32[]{:S(2)}, u32[]{:S(2)}) collective-permute-start(f32[128,128]{1,0:T(8,128)S(1)} %add.182), channel_id=1, source_target_pairs={{0,4},{2,6},{4,0},{6,2},{8,12},{10,14},{12,8},{14,10},{16,20},{18,... | collective-permute-start | bytes 196616 | tf_op jit(solution)/shard_map/ppermute | solution.py:15
  46.5 4.7 %collective-permute-start.2 = (f32[128,128]{1,0:T(8,128)S(1)}, f32[128,128]{1,0:T(8,128)S(1)}, u32[]{:S(2)}, u32[]{:S(2)}) collective-permute-start(f32[128,128]{1,0:T(8,128)S(1)} %add.183), channel_id=1, source_target_pairs={{0,8},{2,10},{4,12},{6,14},{8,0},{10,2},{12,4},{14,6},{16,24},{18,... | collective-permute-start | bytes 196616 | tf_op jit(solution)/shard_map/ppermute | solution.py:15
  47.4 69.2 %all-gather.7.cloned.1.call-start = ((), (), s32[]{:S(2)}) async-start(), calls=%async_computation.6 | async-start | bytes 1572864 | tf_op jit(solution)/shard_map/all_gather | solution.py:30
  51.2 5.8 %collective-permute-start.3 = (f32[128,128]{1,0:T(8,128)S(1)}, f32[128,128]{1,0:T(8,128)S(1)}, u32[]{:S(2)}, u32[]{:S(2)}) collective-permute-start(f32[128,128]{1,0:T(8,128)S(1)} %add.184), channel_id=1, source_target_pairs={{0,16},{2,18},{4,20},{6,22},{8,24},{10,26},{12,28},{14,30},{16,0},... | collective-permute-start | bytes 196616 | tf_op jit(solution)/shard_map/ppermute | solution.py:15
  57.2 4.3 %collective-permute-start.4 = (f32[128,128]{1,0:T(8,128)S(1)}, f32[128,128]{1,0:T(8,128)S(1)}, u32[]{:S(2)}, u32[]{:S(2)}) collective-permute-start(f32[128,128]{1,0:T(8,128)S(1)} %get-tuple-element.37), channel_id=1, source_target_pairs={{0,2},{2,0},{4,6},{6,4},{8,10},{10,8},{12,14},{14,12},{16,18},{18,... | collective-permute-start | bytes 196616 | tf_op jit(solution)/shard_map/ppermute | solution.py:15
  61.4 4.3 %collective-permute-start.5 = (f32[128,128]{1,0:T(8,128)S(1)}, f32[128,128]{1,0:T(8,128)S(1)}, u32[]{:S(2)}, u32[]{:S(2)}) collective-permute-start(f32[128,128]{1,0:T(8,128)S(1)} %add_dynamic-update-slice_fusion.1), channel_id=1, source_target_pairs={{0,4},{2,6},{4,0},{6,2},{8,12},{10,14},{12,8},{14,10},{16,20},{18,... | collective-permute-start | bytes 196616 | tf_op jit(solution)/shard_map/ppermute | solution.py:15
  65.7 4.3 %collective-permute-start.6 = (f32[128,128]{1,0:T(8,128)S(1)}, f32[128,128]{1,0:T(8,128)S(1)}, u32[]{:S(2)}, u32[]{:S(2)}) collective-permute-start(f32[128,128]{1,0:T(8,128)S(1)} %add.188), channel_id=1, source_target_pairs={{0,8},{2,10},{4,12},{6,14},{8,0},{10,2},{12,4},{14,6},{16,24},{18,... | collective-permute-start | bytes 196616 | tf_op jit(solution)/shard_map/ppermute | solution.py:15
  70.1 5.4 %collective-permute-start.7 = (f32[128,128]{1,0:T(8,128)S(1)}, f32[128,128]{1,0:T(8,128)S(1)}, u32[]{:S(2)}, u32[]{:S(2)}) collective-permute-start(f32[128,128]{1,0:T(8,128)S(1)} %add.189), channel_id=1, source_target_pairs={{0,16},{2,18},{4,20},{6,22},{8,24},{10,26},{12,28},{14,30},{16,0},... | collective-permute-start | bytes 196616 | tf_op jit(solution)/shard_map/ppermute | solution.py:15
  95.4 5.5 %collective-permute-start.12 = (bf16[2,256,128]{1,2,0:T(8,128)(2,1)S(1)}, bf16[2,256,128]{1,2,0:T(8,128)(2,1)S(1)}, u32[]{:S(2)}, u32[]{:S(2)}) collective-permute-start(bf16[2,256,128]{1,2,0:T(8,128)(2,1)S(1)} %get-tuple-element.29), channel_id=1, source_target_pairs={{0,2},{2,0},{4,6},{6,4},{8,10},{10,8},{12,14},{14,12},{16,18},{18,... | collective-permute-start | bytes 393224 | tf_op jit(solution)/shard_map/ppermute | solution.py:15
  97.0 93.6 %all-gather.9.cloned.1.call-start = ((), (), s32[]{:S(2)}) async-start(), calls=%async_computation.7 | async-start | bytes 1572864 | tf_op jit(solution)/shard_map/all_gather | solution.py:30
  97.3 6.6 %collective-permute-start.13 = (bf16[2,256,128]{1,2,0:T(8,128)(2,1)}, bf16[2,256,128]{1,2,0:T(8,128)(2,1)}, u32[]{:S(2)}, u32[]{:S(2)}) collective-permute-start(bf16[2,256,128]{1,2,0:T(8,128)(2,1)} %get-tuple-element.32), channel_id=1, source_target_pairs={{0,4},{2,6},{4,0},{6,2},{8,12},{10,14},{12,8},{14,10},{16,20},{18,... | collective-permute-start | bytes 393224 | tf_op jit(solution)/shard_map/ppermute | solution.py:15
  97.8 9.8 %collective-permute-start.14 = (bf16[2,256,128]{1,2,0:T(8,128)(2,1)}, bf16[2,256,128]{1,2,0:T(8,128)(2,1)}, u32[]{:S(2)}, u32[]{:S(2)}) collective-permute-start(bf16[2,256,128]{1,2,0:T(8,128)(2,1)} %get-tuple-element.31), channel_id=1, source_target_pairs={{0,8},{2,10},{4,12},{6,14},{8,0},{10,2},{12,4},{14,6},{16,24},{18,... | collective-permute-start | bytes 393224 | tf_op jit(solution)/shard_map/ppermute | solution.py:15
  97.8 13.6 %collective-permute-start.15 = (bf16[2,256,128]{1,2,0:T(8,128)(2,1)}, bf16[2,256,128]{1,2,0:T(8,128)(2,1)S(1)}, u32[]{:S(2)}, u32[]{:S(2)}) collective-permute-start(bf16[2,256,128]{1,2,0:T(8,128)(2,1)} %get-tuple-element.30), channel_id=1, source_target_pairs={{0,16},{2,18},{4,20},{6,22},{8,24},{10,26},{12,28},{14,30},{16,0},... | collective-permute-start | bytes 393224 | tf_op jit(solution)/shard_map/ppermute | solution.py:15
  141.8 4.4 %collective-permute-start.19 = (f32[128]{0:T(128)S(1)}, f32[128]{0:T(128)S(1)}, u32[]{:S(2)}, u32[]{:S(2)}) collective-permute-start(f32[128]{0:T(128)S(1)} %add.199), channel_id=1, source_target_pairs={{0,16},{2,18},{4,20},{6,22},{8,24},{10,26},{12,28},{14,30},{16,0},... | collective-permute-start | bytes 1544 | tf_op jit(solution)/shard_map/ppermute | solution.py:15
  142.6 4.4 %collective-permute-start.11 = (f32[128]{0:T(128)S(1)}, f32[128]{0:T(128)S(1)}, u32[]{:S(2)}, u32[]{:S(2)}) collective-permute-start(f32[128]{0:T(128)S(1)} %add.194), channel_id=1, source_target_pairs={{0,16},{2,18},{4,20},{6,22},{8,24},{10,26},{12,28},{14,30},{16,0},... | collective-permute-start | bytes 1544 | tf_op jit(solution)/shard_map/ppermute | solution.py:15
  149.2 104.2 %all-gather.11.cloned.1.call-start = ((), (), s32[]{:S(2)}) async-start(), calls=%async_computation.8 | async-start | bytes 1572864 | tf_op jit(solution)/shard_map/all_gather | solution.py:30
  153.3 4.3 %collective-permute-start.20 = (f32[128,128]{1,0:T(8,128)S(1)}, f32[128,128]{1,0:T(8,128)S(1)}, u32[]{:S(2)}, u32[]{:S(2)}) collective-permute-start(f32[128,128]{1,0:T(8,128)S(1)} %scatter_custom_fusion.3), channel_id=1, source_target_pairs={{0,2},{2,0},{4,6},{6,4},{8,10},{10,8},{12,14},{14,12},{16,18},{18,... | collective-permute-start | bytes 196616 | tf_op jit(solution)/shard_map/ppermute | solution.py:15
  157.7 4.3 %collective-permute-start.21 = (f32[128,128]{1,0:T(8,128)S(1)}, f32[128,128]{1,0:T(8,128)S(1)}, u32[]{:S(2)}, u32[]{:S(2)}) collective-permute-start(f32[128,128]{1,0:T(8,128)S(1)} %add.201), channel_id=1, source_target_pairs={{0,4},{2,6},{4,0},{6,2},{8,12},{10,14},{12,8},{14,10},{16,20},{18,... | collective-permute-start | bytes 196616 | tf_op jit(solution)/shard_map/ppermute | solution.py:15
  162.0 4.3 %collective-permute-start.22 = (f32[128,128]{1,0:T(8,128)S(1)}, f32[128,128]{1,0:T(8,128)S(1)}, u32[]{:S(2)}, u32[]{:S(2)}) collective-permute-start(f32[128,128]{1,0:T(8,128)S(1)} %add.202), channel_id=1, source_target_pairs={{0,8},{2,10},{4,12},{6,14},{8,0},{10,2},{12,4},{14,6},{16,24},{18,... | collective-permute-start | bytes 196616 | tf_op jit(solution)/shard_map/ppermute | solution.py:15
  166.3 5.2 %collective-permute-start.23 = (f32[128,128]{1,0:T(8,128)S(1)}, f32[128,128]{1,0:T(8,128)S(1)}, u32[]{:S(2)}, u32[]{:S(2)}) collective-permute-start(f32[128,128]{1,0:T(8,128)S(1)} %add.203), channel_id=1, source_target_pairs={{0,16},{2,18},{4,20},{6,22},{8,24},{10,26},{12,28},{14,30},{16,0},... | collective-permute-start | bytes 196616 | tf_op jit(solution)/shard_map/ppermute | solution.py:15
  171.7 4.3 %collective-permute-start.24 = (f32[128,128]{1,0:T(8,128)S(1)}, f32[128,128]{1,0:T(8,128)S(1)}, u32[]{:S(2)}, u32[]{:S(2)}) collective-permute-start(f32[128,128]{1,0:T(8,128)S(1)} %get-tuple-element.39), channel_id=1, source_target_pairs={{0,2},{2,0},{4,6},{6,4},{8,10},{10,8},{12,14},{14,12},{16,18},{18,... | collective-permute-start | bytes 196616 | tf_op jit(solution)/shard_map/ppermute | solution.py:15
  180.3 4.3 %collective-permute-start.26 = (f32[128,128]{1,0:T(8,128)S(1)}, f32[128,128]{1,0:T(8,128)S(1)}, u32[]{:S(2)}, u32[]{:S(2)}) collective-permute-start(f32[128,128]{1,0:T(8,128)S(1)} %add.206), channel_id=1, source_target_pairs={{0,8},{2,10},{4,12},{6,14},{8,0},{10,2},{12,4},{14,6},{16,24},{18,... | collective-permute-start | bytes 196616 | tf_op jit(solution)/shard_map/ppermute | solution.py:15
  184.7 5.2 %collective-permute-start.27 = (f32[128,128]{1,0:T(8,128)S(1)}, f32[128,128]{1,0:T(8,128)S(1)}, u32[]{:S(2)}, u32[]{:S(2)}) collective-permute-start(f32[128,128]{1,0:T(8,128)S(1)} %add.207), channel_id=1, source_target_pairs={{0,16},{2,18},{4,20},{6,22},{8,24},{10,26},{12,28},{14,30},{16,0},... | collective-permute-start | bytes 196616 | tf_op jit(solution)/shard_map/ppermute | solution.py:15
  225.1 4.4 %collective-permute-start.31 = (f32[128]{0:T(128)S(1)}, f32[128]{0:T(128)S(1)}, u32[]{:S(2)}, u32[]{:S(2)}) collective-permute-start(f32[128]{0:T(128)S(1)} %add.211), channel_id=1, source_target_pairs={{0,16},{2,18},{4,20},{6,22},{8,24},{10,26},{12,28},{14,30},{16,0},... | collective-permute-start | bytes 1544 | tf_op jit(solution)/shard_map/ppermute | solution.py:15
  232.4 5.3 %collective-permute-start.32 = (bf16[2,256,128]{1,2,0:T(8,128)(2,1)S(1)}, bf16[2,256,128]{1,2,0:T(8,128)(2,1)S(1)}, u32[]{:S(2)}, u32[]{:S(2)}) collective-permute-start(bf16[2,256,128]{1,2,0:T(8,128)(2,1)S(1)} %get-tuple-element.21), channel_id=1, source_target_pairs={{0,2},{2,0},{4,6},{6,4},{8,10},{10,8},{12,14},{14,12},{16,18},{18,... | collective-permute-start | bytes 393224 | tf_op jit(solution)/shard_map/ppermute | solution.py:15
  233.6 7.0 %collective-permute-start.33 = (bf16[2,256,128]{1,2,0:T(8,128)(2,1)}, bf16[2,256,128]{1,2,0:T(8,128)(2,1)}, u32[]{:S(2)}, u32[]{:S(2)}) collective-permute-start(bf16[2,256,128]{1,2,0:T(8,128)(2,1)} %get-tuple-element.24), channel_id=1, source_target_pairs={{0,4},{2,6},{4,0},{6,2},{8,12},{10,14},{12,8},{14,10},{16,20},{18,... | collective-permute-start | bytes 393224 | tf_op jit(solution)/shard_map/ppermute | solution.py:15
  234.5 9.9 %collective-permute-start.34 = (bf16[2,256,128]{1,2,0:T(8,128)(2,1)}, bf16[2,256,128]{1,2,0:T(8,128)(2,1)}, u32[]{:S(2)}, u32[]{:S(2)}) collective-permute-start(bf16[2,256,128]{1,2,0:T(8,128)(2,1)} %get-tuple-element.23), channel_id=1, source_target_pairs={{0,8},{2,10},{4,12},{6,14},{8,0},{10,2},{12,4},{14,6},{16,24},{18,... | collective-permute-start | bytes 393224 | tf_op jit(solution)/shard_map/ppermute | solution.py:15
  236.3 11.9 %collective-permute-start.35 = (bf16[2,256,128]{1,2,0:T(8,128)(2,1)}, bf16[2,256,128]{1,2,0:T(8,128)(2,1)S(1)}, u32[]{:S(2)}, u32[]{:S(2)}) collective-permute-start(bf16[2,256,128]{1,2,0:T(8,128)(2,1)} %get-tuple-element.22), channel_id=1, source_target_pairs={{0,16},{2,18},{4,20},{6,22},{8,24},{10,26},{12,28},{14,30},{16,0},... | collective-permute-start | bytes 393224 | tf_op jit(solution)/shard_map/ppermute | solution.py:15
  278.5 4.4 %collective-permute-start.39 = (f32[128]{0:T(128)S(1)}, f32[128]{0:T(128)S(1)}, u32[]{:S(2)}, u32[]{:S(2)}) collective-permute-start(f32[128]{0:T(128)S(1)} %add.217), channel_id=1, source_target_pairs={{0,16},{2,18},{4,20},{6,22},{8,24},{10,26},{12,28},{14,30},{16,0},... | collective-permute-start | bytes 1544 | tf_op jit(solution)/shard_map/ppermute | solution.py:15
  (35 other events, 476.3 us)
Sparse Core Ops, SparseCore 0:
  47.5 6.6 all-gather.4
  97.2 7.4 all-gather.6
  149.3 7.6 all-gather.8
  233.7 9.0 all-gather.10
where the time goes:
time: 295 us; the launch traced here: 293 us
  waiting for transfers between devices  86.9 us (29%)
  local copies, waits for them, and re-layouts  67.7 us (23%)
  starting transfers between devices  55.6 us (19%)
  other arithmetic  29.9 us (10%)
  matrix products  21.3 us (7%)
  blocking collectives  18.3 us (6%)
  between operations  13.5 us (5%)
    ppermute x40, waiting for transfers between devices, swapped(): lax.ppermute(shard, axis, [(i, i ^ 1 << distance) for i in range(lax.axis...  82.5 us
    ppermute x40, starting transfers between devices, swapped(): lax.ppermute(shard, axis, [(i, i ^ 1 << distance) for i in range(lax.axis...  46.9 us
    all_to_all x4, blocking collectives, schur_apply(): lax.all_to_all(half_rows, 'rhs', split_axis=2, concat_axis=1, tiled=True)  18.3 us
    all_to_all x8, local copies, waits for them, and re-layouts, schur_apply(): lax.all_to_all(half_rows, 'rhs', split_axis=2, concat_axis=1, tiled=True)  17.4 us
    dot_general x8, matrix products, jump_terms(): jnp.einsum('sj,jfc->sfc', select, partner_face, preferred_element_type=jn...  10.1 us
    ppermute x8, local copies, waits for them, and re-layouts, swapped(): lax.ppermute(shard, axis, [(i, i ^ 1 << distance) for i in range(lax.axis...  9.77 us
    all_to_all x1, starting transfers between devices, on_device(): lax.all_to_all(buffer, 'sub', split_axis=0, concat_axis=0, tiled=True)  8.35 us
    dot_general x4, matrix products, schur_apply(): jnp.einsum('snm,smc->snc', schur_block, lax.all_gather(rounded, 'rhs', ax...  7.88 us
  transfers between devices with their start and end apart: 45, of which 34 were waited for; matrix products, arithmetic and copies ran while one was open for 14% of the time, Pallas kernels for 0%

commit v1 on v0

--- a/solution.py
+++ b/solution.py
@@ -30,7 +30,10 @@
         lax.all_gather(rounded, "rhs", axis=2, tiled=True),
         preferred_element_type=jnp.float32,
     )
-    return lax.all_to_all(half_rows, "rhs", split_axis=2, concat_axis=1, tiled=True)
+    return jnp.concatenate(
+        lax.all_to_all(jnp.stack(jnp.split(half_rows, lax.axis_size("rhs"), axis=2)), "rhs", 0, 0),
+        axis=1,
+    )
 
 
 def jump_terms(rounded, partner_slot):

time: 295 us -> 269 us (0.912)
  local copies, waits for them, and re-layouts: 67.7 us -> 47.7 us
  other arithmetic: 29.9 us -> 24.3 us
    all_to_all x8 -> x0, local copies, waits for them, and re-layouts: 17.4 us -> none  [schur_apply(): lax.all_to_all(half_rows, 'rhs', split_axis=2, concat_axis=1, tiled=True)]
    reduce_sum x2, other arithmetic: 4.38 us -> 0.78 us  [on_device(): curvature = all_sum(jnp.sum(direction * applied, axis=(0, 1)))]
    dot_general x4 -> x0, local copies, waits for them, and re-layouts: 3.24 us -> none  [schur_apply(): jnp.einsum('snm,smc->snc', schur_block, lax.all_gather(rounded, 'rhs', ax...]
  transfers between devices with their start and end apart: 45 -> 45, of which waited for: 34 -> 35; matrix products, arithmetic and copies ran while one was open for 14% -> 16% of each run, Pallas kernels for 0% -> 0%
where the time goes in v1:
time: 269 us; the launch traced here: 268 us
  waiting for transfers between devices  88.4 us (33%)
  starting transfers between devices  53.8 us (20%)
  local copies, waits for them, and re-layouts  47.7 us (18%)
  other arithmetic  24.3 us (9%)
  matrix products  21.3 us (8%)
  blocking collectives  18.6 us (7%)
  between operations  13.7 us (5%)
    ppermute x40, waiting for transfers between devices, swapped(): lax.ppermute(shard, axis, [(i, i ^ 1 << distance) for i in range(lax.axis...  83.9 us
    ppermute x40, starting transfers between devices, swapped(): lax.ppermute(shard, axis, [(i, i ^ 1 << distance) for i in range(lax.axis...  45.3 us
    all_to_all x4, blocking collectives, schur_apply(): lax.all_to_all(jnp.stack(jnp.split(half_rows, lax.axis_size('rhs'), axis=...  18.6 us
    dot_general x8, matrix products, jump_terms(): jnp.einsum('sj,jfc->sfc', select, partner_face, preferred_element_type=jn...  10.1 us
    ppermute x8, local copies, waits for them, and re-layouts, swapped(): lax.ppermute(shard, axis, [(i, i ^ 1 << distance) for i in range(lax.axis...  9.79 us
    all_to_all x1, starting transfers between devices, on_device(): lax.all_to_all(buffer, 'sub', split_axis=0, concat_axis=0, tiled=True)  8.38 us
    dot_general x4, matrix products, schur_apply(): jnp.einsum('snm,smc->snc', schur_block, lax.all_gather(rounded, 'rhs', ax...  7.88 us
    scatter x1, local copies, waits for them, and re-layouts, on_device(): buffer = jnp.zeros((all_subdomains * MOST, points, columns), jnp.bfloat16...  6.77 us
  transfers between devices with their start and end apart: 45, of which 35 were waited for; matrix products, arithmetic and copies ran while one was open for 16% of the time, Pallas kernels for 0%

profile of v1, /device:TPU:0, one launch (start us, length us, event | category | flops | bytes accessed | tf_op | source)
XLA Modules:
  0.0 267.8 jit_solution(15398155675783967642)
XLA Ops:
  8.9 6.8 %scatter_fusion = bf16[128,4,128]{2,1,0:T(4,128)(2,1)} fusion(bf16[128,4,128]{2,1,0:T(4,128)(2,1)} %broadcast_in_dim.12, s32[64]{0:T(128)S(1)} %fusion.24, bf16[64,4,128]{2,1,0:T(4,128)(2,1)} %param.13), kind=kCustom, calls=%fused_computation.4 | custom fusion | bytes 196864 | tf_op jit(solution)/shard_map/scatter | solution.py:111
  15.7 8.4 %all-to-all-start = ((bf16[128,4,128]{2,1,0:T(4,128)(2,1)}), bf16[128,4,128]{2,1,0:T(4,128)(2,1)S(1)}, u32[]{:S(2)}, u32[]{:S(2)}) async-start(bf16[128,4,128]{2,1,0:T(4,128)(2,1)} %scatter_fusion), calls=%async_computation | async-start | bytes 262144 | tf_op jit(solution)/shard_map/all_to_all | solution.py:113
  24.8 2.5 copy.70
  27.5 4.4 %all-to-all-done = bf16[128,4,128]{2,1,0:T(4,128)(2,1)S(1)} async-done(((bf16[128,4,128]{2,1,0:T(4,128)(2,1)}), bf16[128,4,128]{2,1,0:T(4,128)(2,1)S(1)}, u32[]{:S(2)}, u32[]{:S(2)}) %all-to-all-start) | async-done | bytes 131104 | tf_op jit(solution)/shard_map/all_to_all | solution.py:113
  32.0 3.1 %multiply_convert_fusion.1 = (bf16[2,1024,128]{1,2,0:T(8,128)(2,1)}, f32[2,1024,128]{1,2,0:T(8,128)S(1)}) fusion(f32[2,1024]{1,0:T(2,128)S(1)} %copy-done.11, f32[2,1024,128]{1,2,0:T(8,128)} %copy.70, f32[2,4,128]{2,1,0:T(4,128)S(1)} %convert_reduce_fusion, f32[4,1024]{1,0:T(4,128)S(1)} %copy-done.14), kind=kOutput, calls=%fused_computation.32 | convolution fusion | flops 13369344 | bytes 2650112 | tf_op jit(solution)/shard_map/pm,spc->smc/dot_general | solution.py:117
  39.0 3.2 %collective-permute-done = f32[128,128]{1,0:T(8,128)S(1)} collective-permute-done((f32[128,128]{1,0:T(8,128)S(1)}, f32[128,128]{1,0:T(8,128)S(1)}, u32[]{:S(2)}, u32[]{:S(2)}) %collective-permute-start) | collective-permute-done | bytes 65568 | tf_op jit(solution)/shard_map/ppermute | solution.py:15
  43.0 3.5 %collective-permute-done.1 = f32[128,128]{1,0:T(8,128)S(1)} collective-permute-done((f32[128,128]{1,0:T(8,128)S(1)}, f32[128,128]{1,0:T(8,128)S(1)}, u32[]{:S(2)}, u32[]{:S(2)}) %collective-permute-start.1) | collective-permute-done | bytes 65568 | tf_op jit(solution)/shard_map/ppermute | solution.py:15
  47.4 3.8 %collective-permute-done.2 = f32[128,128]{1,0:T(8,128)S(1)} collective-permute-done((f32[128,128]{1,0:T(8,128)S(1)}, f32[128,128]{1,0:T(8,128)S(1)}, u32[]{:S(2)}, u32[]{:S(2)}) %collective-permute-start.2) | collective-permute-done | bytes 65568 | tf_op jit(solution)/shard_map/ppermute | solution.py:15
  52.0 5.0 %collective-permute-done.3 = f32[128,128]{1,0:T(8,128)S(1)} collective-permute-done((f32[128,128]{1,0:T(8,128)S(1)}, f32[128,128]{1,0:T(8,128)S(1)}, u32[]{:S(2)}, u32[]{:S(2)}) %collective-permute-start.3) | collective-permute-done | bytes 65568 | tf_op jit(solution)/shard_map/ppermute | solution.py:15
  58.0 3.4 %collective-permute-done.4 = f32[128,128]{1,0:T(8,128)S(1)} collective-permute-done((f32[128,128]{1,0:T(8,128)S(1)}, f32[128,128]{1,0:T(8,128)S(1)}, u32[]{:S(2)}, u32[]{:S(2)}) %collective-permute-start.4) | collective-permute-done | bytes 65568 | tf_op jit(solution)/shard_map/ppermute | solution.py:15
  62.2 3.5 %collective-permute-done.5 = f32[128,128]{1,0:T(8,128)S(1)} collective-permute-done((f32[128,128]{1,0:T(8,128)S(1)}, f32[128,128]{1,0:T(8,128)S(1)}, u32[]{:S(2)}, u32[]{:S(2)}) %collective-permute-start.5) | collective-permute-done | bytes 65568 | tf_op jit(solution)/shard_map/ppermute | solution.py:15
  66.0 4.1 %collective-permute-done.6 = f32[128,128]{1,0:T(8,128)S(1)} collective-permute-done((f32[128,128]{1,0:T(8,128)S(1)}, f32[128,128]{1,0:T(8,128)S(1)}, u32[]{:S(2)}, u32[]{:S(2)}) %collective-permute-start.6) | collective-permute-done | bytes 65568 | tf_op jit(solution)/shard_map/ppermute | solution.py:15
  70.4 5.1 %collective-permute-done.7 = f32[128,128]{1,0:T(8,128)S(1)} collective-permute-done((f32[128,128]{1,0:T(8,128)S(1)}, f32[128,128]{1,0:T(8,128)S(1)}, u32[]{:S(2)}, u32[]{:S(2)}) %collective-permute-start.7) | collective-permute-done | bytes 65568 | tf_op jit(solution)/shard_map/ppermute | solution.py:15
  78.2 4.6 %all_to_all.25 = f32[2,2,512,128]{2,3,1,0:T(8,128)S(1)} all-to-all(f32[2,2,512,128]{2,3,1,0:T(8,128)S(1)} %pad_maximum_fusion), channel_id=1, replica_groups=mesh['sub'=16,'rhs'=2] {'rhs'}, dimensions={0} | all-to-all | bytes 2097152 | tf_op jit(solution)/shard_map/all_to_all | solution.py:34
  109.8 2.3 subtract_multiply_fusion.7
  114.4 4.7 %all_to_all.26 = f32[2,2,512,128]{2,3,1,0:T(8,128)S(1)} all-to-all(f32[2,2,512,128]{2,3,1,0:T(8,128)S(1)} %pad_maximum_fusion.1), channel_id=1, replica_groups=mesh['sub'=16,'rhs'=2] {'rhs'}, dimensions={0} | all-to-all | bytes 2097152 | tf_op jit(solution)/shard_map/all_to_all | solution.py:34
  137.6 2.6 copy.88
  143.1 3.1 %collective-permute-done.20 = f32[128,128]{1,0:T(8,128)S(1)} collective-permute-done((f32[128,128]{1,0:T(8,128)S(1)}, f32[128,128]{1,0:T(8,128)S(1)}, u32[]{:S(2)}, u32[]{:S(2)}) %collective-permute-start.20) | collective-permute-done | bytes 65568 | tf_op jit(solution)/shard_map/ppermute | solution.py:15
  147.5 3.1 %collective-permute-done.21 = f32[128,128]{1,0:T(8,128)S(1)} collective-permute-done((f32[128,128]{1,0:T(8,128)S(1)}, f32[128,128]{1,0:T(8,128)S(1)}, u32[]{:S(2)}, u32[]{:S(2)}) %collective-permute-start.21) | collective-permute-done | bytes 65568 | tf_op jit(solution)/shard_map/ppermute | solution.py:15
  152.1 2.8 %collective-permute-done.22 = f32[128,128]{1,0:T(8,128)S(1)} collective-permute-done((f32[128,128]{1,0:T(8,128)S(1)}, f32[128,128]{1,0:T(8,128)S(1)}, u32[]{:S(2)}, u32[]{:S(2)}) %collective-permute-start.22) | collective-permute-done | bytes 65568 | tf_op jit(solution)/shard_map/ppermute | solution.py:15
  157.1 3.1 %collective-permute-done.23 = f32[128,128]{1,0:T(8,128)S(1)} collective-permute-done((f32[128,128]{1,0:T(8,128)S(1)}, f32[128,128]{1,0:T(8,128)S(1)}, u32[]{:S(2)}, u32[]{:S(2)}) %collective-permute-start.23) | collective-permute-done | bytes 65568 | tf_op jit(solution)/shard_map/ppermute | solution.py:15
  161.5 3.1 %collective-permute-done.24 = f32[128,128]{1,0:T(8,128)S(1)} collective-permute-done((f32[128,128]{1,0:T(8,128)S(1)}, f32[128,128]{1,0:T(8,128)S(1)}, u32[]{:S(2)}, u32[]{:S(2)}) %collective-permute-start.24) | collective-permute-done | bytes 65568 | tf_op jit(solution)/shard_map/ppermute | solution.py:15
  165.8 3.1 %collective-permute-done.25 = f32[128,128]{1,0:T(8,128)S(1)} collective-permute-done((f32[128,128]{1,0:T(8,128)S(1)}, f32[128,128]{1,0:T(8,128)S(1)}, u32[]{:S(2)}, u32[]{:S(2)}) %collective-permute-start.25) | collective-permute-done | bytes 65568 | tf_op jit(solution)/shard_map/ppermute | solution.py:15
  170.4 2.8 %collective-permute-done.26 = f32[128,128]{1,0:T(8,128)S(1)} collective-permute-done((f32[128,128]{1,0:T(8,128)S(1)}, f32[128,128]{1,0:T(8,128)S(1)}, u32[]{:S(2)}, u32[]{:S(2)}) %collective-permute-start.26) | collective-permute-done | bytes 65568 | tf_op jit(solution)/shard_map/ppermute | solution.py:15
  175.4 3.1 %collective-permute-done.27 = f32[128,128]{1,0:T(8,128)S(1)} collective-permute-done((f32[128,128]{1,0:T(8,128)S(1)}, f32[128,128]{1,0:T(8,128)S(1)}, u32[]{:S(2)}, u32[]{:S(2)}) %collective-permute-start.27) | collective-permute-done | bytes 65568 | tf_op jit(solution)/shard_map/ppermute | solution.py:15
  181.3 4.6 %all_to_all.27 = f32[2,2,512,128]{2,3,1,0:T(8,128)S(1)} all-to-all(f32[2,2,512,128]{2,3,1,0:T(8,128)S(1)} %pad_maximum_fusion.2), channel_id=1, replica_groups=mesh['sub'=16,'rhs'=2] {'rhs'}, dimensions={0} | all-to-all | bytes 2097152 | tf_op jit(solution)/shard_map/all_to_all | solution.py:34
  187.1 2.5 copy.89
  191.9 2.5 copy.90
  201.0 2.4 collective-permute-done.29
  209.0 2.4 collective-permute-done.31
  237.1 4.7 %all_to_all.28 = f32[2,2,512,128]{2,3,1,0:T(8,128)S(1)} all-to-all(f32[2,2,512,128]{2,3,1,0:T(8,128)S(1)} %pad_maximum_fusion.3), channel_id=1, replica_groups=mesh['sub'=16,'rhs'=2] {'rhs'}, dimensions={0} | all-to-all | bytes 2097152 | tf_op jit(solution)/shard_map/all_to_all | solution.py:34
  258.8 2.5 copy.102
  (230 shorter events, 137.5 us)
Async XLA Ops:
  15.7 16.2 %all-to-all-start = ((bf16[128,4,128]{2,1,0:T(4,128)(2,1)}), bf16[128,4,128]{2,1,0:T(4,128)(2,1)S(1)}, u32[]{:S(2)}, u32[]{:S(2)}) async-start(bf16[128,4,128]{2,1,0:T(4,128)(2,1)} %scatter_fusion), calls=%async_computation | async-start | bytes 262144 | tf_op jit(solution)/shard_map/all_to_all | solution.py:113
  24.1 52.0 %all-gather.5.cloned.1.call-start = ((), (), s32[]{:S(2)}) async-start(), calls=%async_computation.5 | async-start | bytes 1572864 | tf_op jit(solution)/shard_map/all_gather | solution.py:30
  37.9 4.3 %collective-permute-start = (f32[128,128]{1,0:T(8,128)S(1)}, f32[128,128]{1,0:T(8,128)S(1)}, u32[]{:S(2)}, u32[]{:S(2)}) collective-permute-start(f32[128,128]{1,0:T(8,128)S(1)} %scatter_custom_fusion.1), channel_id=1, source_target_pairs={{0,2},{2,0},{4,6},{6,4},{8,10},{10,8},{12,14},{14,12},{16,18},{18,... | collective-permute-start | bytes 196616 | tf_op jit(solution)/shard_map/ppermute | solution.py:15
  42.2 4.3 %collective-permute-start.1 = (f32[128,128]{1,0:T(8,128)S(1)}, f32[128,128]{1,0:T(8,128)S(1)}, u32[]{:S(2)}, u32[]{:S(2)}) collective-permute-start(f32[128,128]{1,0:T(8,128)S(1)} %add.182), channel_id=1, source_target_pairs={{0,4},{2,6},{4,0},{6,2},{8,12},{10,14},{12,8},{14,10},{16,20},{18,... | collective-permute-start | bytes 196616 | tf_op jit(solution)/shard_map/ppermute | solution.py:15
  46.6 4.7 %collective-permute-start.2 = (f32[128,128]{1,0:T(8,128)S(1)}, f32[128,128]{1,0:T(8,128)S(1)}, u32[]{:S(2)}, u32[]{:S(2)}) collective-permute-start(f32[128,128]{1,0:T(8,128)S(1)} %add.183), channel_id=1, source_target_pairs={{0,8},{2,10},{4,12},{6,14},{8,0},{10,2},{12,4},{14,6},{16,24},{18,... | collective-permute-start | bytes 196616 | tf_op jit(solution)/shard_map/ppermute | solution.py:15
  47.4 64.8 %all-gather.7.cloned.1.call-start = ((), (), s32[]{:S(2)}) async-start(), calls=%async_computation.6 | async-start | bytes 1572864 | tf_op jit(solution)/shard_map/all_gather | solution.py:30
  51.2 5.8 %collective-permute-start.3 = (f32[128,128]{1,0:T(8,128)S(1)}, f32[128,128]{1,0:T(8,128)S(1)}, u32[]{:S(2)}, u32[]{:S(2)}) collective-permute-start(f32[128,128]{1,0:T(8,128)S(1)} %add.184), channel_id=1, source_target_pairs={{0,16},{2,18},{4,20},{6,22},{8,24},{10,26},{12,28},{14,30},{16,0},... | collective-permute-start | bytes 196616 | tf_op jit(solution)/shard_map/ppermute | solution.py:15
  57.2 4.3 %collective-permute-start.4 = (f32[128,128]{1,0:T(8,128)S(1)}, f32[128,128]{1,0:T(8,128)S(1)}, u32[]{:S(2)}, u32[]{:S(2)}) collective-permute-start(f32[128,128]{1,0:T(8,128)S(1)} %get-tuple-element.45), channel_id=1, source_target_pairs={{0,2},{2,0},{4,6},{6,4},{8,10},{10,8},{12,14},{14,12},{16,18},{18,... | collective-permute-start | bytes 196616 | tf_op jit(solution)/shard_map/ppermute | solution.py:15
  61.5 4.3 %collective-permute-start.5 = (f32[128,128]{1,0:T(8,128)S(1)}, f32[128,128]{1,0:T(8,128)S(1)}, u32[]{:S(2)}, u32[]{:S(2)}) collective-permute-start(f32[128,128]{1,0:T(8,128)S(1)} %add_dynamic-update-slice_fusion.1), channel_id=1, source_target_pairs={{0,4},{2,6},{4,0},{6,2},{8,12},{10,14},{12,8},{14,10},{16,20},{18,... | collective-permute-start | bytes 196616 | tf_op jit(solution)/shard_map/ppermute | solution.py:15
  65.8 4.3 %collective-permute-start.6 = (f32[128,128]{1,0:T(8,128)S(1)}, f32[128,128]{1,0:T(8,128)S(1)}, u32[]{:S(2)}, u32[]{:S(2)}) collective-permute-start(f32[128,128]{1,0:T(8,128)S(1)} %add.188), channel_id=1, source_target_pairs={{0,8},{2,10},{4,12},{6,14},{8,0},{10,2},{12,4},{14,6},{16,24},{18,... | collective-permute-start | bytes 196616 | tf_op jit(solution)/shard_map/ppermute | solution.py:15
  70.1 5.4 %collective-permute-start.7 = (f32[128,128]{1,0:T(8,128)S(1)}, f32[128,128]{1,0:T(8,128)S(1)}, u32[]{:S(2)}, u32[]{:S(2)}) collective-permute-start(f32[128,128]{1,0:T(8,128)S(1)} %add.189), channel_id=1, source_target_pairs={{0,16},{2,18},{4,20},{6,22},{8,24},{10,26},{12,28},{14,30},{16,0},... | collective-permute-start | bytes 196616 | tf_op jit(solution)/shard_map/ppermute | solution.py:15
  91.0 5.5 %collective-permute-start.12 = (bf16[2,256,128]{1,2,0:T(8,128)(2,1)S(1)}, bf16[2,256,128]{1,2,0:T(8,128)(2,1)S(1)}, u32[]{:S(2)}, u32[]{:S(2)}) collective-permute-start(bf16[2,256,128]{1,2,0:T(8,128)(2,1)S(1)} %get-tuple-element.37), channel_id=1, source_target_pairs={{0,2},{2,0},{4,6},{6,4},{8,10},{10,8},{12,14},{14,12},{16,18},{18,... | collective-permute-start | bytes 393224 | tf_op jit(solution)/shard_map/ppermute | solution.py:15
  92.6 86.6 %all-gather.9.cloned.1.call-start = ((), (), s32[]{:S(2)}) async-start(), calls=%async_computation.7 | async-start | bytes 1572864 | tf_op jit(solution)/shard_map/all_gather | solution.py:30
  92.7 6.7 %collective-permute-start.13 = (bf16[2,256,128]{1,2,0:T(8,128)(2,1)}, bf16[2,256,128]{1,2,0:T(8,128)(2,1)}, u32[]{:S(2)}, u32[]{:S(2)}) collective-permute-start(bf16[2,256,128]{1,2,0:T(8,128)(2,1)} %get-tuple-element.40), channel_id=1, source_target_pairs={{0,4},{2,6},{4,0},{6,2},{8,12},{10,14},{12,8},{14,10},{16,20},{18,... | collective-permute-start | bytes 393224 | tf_op jit(solution)/shard_map/ppermute | solution.py:15
  93.2 10.0 %collective-permute-start.14 = (bf16[2,256,128]{1,2,0:T(8,128)(2,1)}, bf16[2,256,128]{1,2,0:T(8,128)(2,1)}, u32[]{:S(2)}, u32[]{:S(2)}) collective-permute-start(bf16[2,256,128]{1,2,0:T(8,128)(2,1)} %get-tuple-element.39), channel_id=1, source_target_pairs={{0,8},{2,10},{4,12},{6,14},{8,0},{10,2},{12,4},{14,6},{16,24},{18,... | collective-permute-start | bytes 393224 | tf_op jit(solution)/shard_map/ppermute | solution.py:15
  93.2 13.8 %collective-permute-start.15 = (bf16[2,256,128]{1,2,0:T(8,128)(2,1)}, bf16[2,256,128]{1,2,0:T(8,128)(2,1)S(1)}, u32[]{:S(2)}, u32[]{:S(2)}) collective-permute-start(bf16[2,256,128]{1,2,0:T(8,128)(2,1)} %get-tuple-element.38), channel_id=1, source_target_pairs={{0,16},{2,18},{4,20},{6,22},{8,24},{10,26},{12,28},{14,30},{16,0},... | collective-permute-start | bytes 393224 | tf_op jit(solution)/shard_map/ppermute | solution.py:15
  130.3 4.4 %collective-permute-start.19 = (f32[128]{0:T(128)S(1)}, f32[128]{0:T(128)S(1)}, u32[]{:S(2)}, u32[]{:S(2)}) collective-permute-start(f32[128]{0:T(128)S(1)} %add.199), channel_id=1, source_target_pairs={{0,16},{2,18},{4,20},{6,22},{8,24},{10,26},{12,28},{14,30},{16,0},... | collective-permute-start | bytes 1544 | tf_op jit(solution)/shard_map/ppermute | solution.py:15
  131.1 4.4 %collective-permute-start.11 = (f32[128]{0:T(128)S(1)}, f32[128]{0:T(128)S(1)}, u32[]{:S(2)}, u32[]{:S(2)}) collective-permute-start(f32[128]{0:T(128)S(1)} %add.194), channel_id=1, source_target_pairs={{0,16},{2,18},{4,20},{6,22},{8,24},{10,26},{12,28},{14,30},{16,0},... | collective-permute-start | bytes 1544 | tf_op jit(solution)/shard_map/ppermute | solution.py:15
  137.5 97.3 %all-gather.11.cloned.1.call-start = ((), (), s32[]{:S(2)}) async-start(), calls=%async_computation.8 | async-start | bytes 1572864 | tf_op jit(solution)/shard_map/all_gather | solution.py:30
  141.9 4.3 %collective-permute-start.20 = (f32[128,128]{1,0:T(8,128)S(1)}, f32[128,128]{1,0:T(8,128)S(1)}, u32[]{:S(2)}, u32[]{:S(2)}) collective-permute-start(f32[128,128]{1,0:T(8,128)S(1)} %scatter_custom_fusion.3), channel_id=1, source_target_pairs={{0,2},{2,0},{4,6},{6,4},{8,10},{10,8},{12,14},{14,12},{16,18},{18,... | collective-permute-start | bytes 196616 | tf_op jit(solution)/shard_map/ppermute | solution.py:15
  146.2 4.3 %collective-permute-start.21 = (f32[128,128]{1,0:T(8,128)S(1)}, f32[128,128]{1,0:T(8,128)S(1)}, u32[]{:S(2)}, u32[]{:S(2)}) collective-permute-start(f32[128,128]{1,0:T(8,128)S(1)} %add.201), channel_id=1, source_target_pairs={{0,4},{2,6},{4,0},{6,2},{8,12},{10,14},{12,8},{14,10},{16,20},{18,... | collective-permute-start | bytes 196616 | tf_op jit(solution)/shard_map/ppermute | solution.py:15
  150.6 4.3 %collective-permute-start.22 = (f32[128,128]{1,0:T(8,128)S(1)}, f32[128,128]{1,0:T(8,128)S(1)}, u32[]{:S(2)}, u32[]{:S(2)}) collective-permute-start(f32[128,128]{1,0:T(8,128)S(1)} %add.202), channel_id=1, source_target_pairs={{0,8},{2,10},{4,12},{6,14},{8,0},{10,2},{12,4},{14,6},{16,24},{18,... | collective-permute-start | bytes 196616 | tf_op jit(solution)/shard_map/ppermute | solution.py:15
  154.9 5.2 %collective-permute-start.23 = (f32[128,128]{1,0:T(8,128)S(1)}, f32[128,128]{1,0:T(8,128)S(1)}, u32[]{:S(2)}, u32[]{:S(2)}) collective-permute-start(f32[128,128]{1,0:T(8,128)S(1)} %add.203), channel_id=1, source_target_pairs={{0,16},{2,18},{4,20},{6,22},{8,24},{10,26},{12,28},{14,30},{16,0},... | collective-permute-start | bytes 196616 | tf_op jit(solution)/shard_map/ppermute | solution.py:15
  160.3 4.3 %collective-permute-start.24 = (f32[128,128]{1,0:T(8,128)S(1)}, f32[128,128]{1,0:T(8,128)S(1)}, u32[]{:S(2)}, u32[]{:S(2)}) collective-permute-start(f32[128,128]{1,0:T(8,128)S(1)} %get-tuple-element.47), channel_id=1, source_target_pairs={{0,2},{2,0},{4,6},{6,4},{8,10},{10,8},{12,14},{14,12},{16,18},{18,... | collective-permute-start | bytes 196616 | tf_op jit(solution)/shard_map/ppermute | solution.py:15
  168.9 4.3 %collective-permute-start.26 = (f32[128,128]{1,0:T(8,128)S(1)}, f32[128,128]{1,0:T(8,128)S(1)}, u32[]{:S(2)}, u32[]{:S(2)}) collective-permute-start(f32[128,128]{1,0:T(8,128)S(1)} %add.206), channel_id=1, source_target_pairs={{0,8},{2,10},{4,12},{6,14},{8,0},{10,2},{12,4},{14,6},{16,24},{18,... | collective-permute-start | bytes 196616 | tf_op jit(solution)/shard_map/ppermute | solution.py:15
  173.2 5.2 %collective-permute-start.27 = (f32[128,128]{1,0:T(8,128)S(1)}, f32[128,128]{1,0:T(8,128)S(1)}, u32[]{:S(2)}, u32[]{:S(2)}) collective-permute-start(f32[128,128]{1,0:T(8,128)S(1)} %add.207), channel_id=1, source_target_pairs={{0,16},{2,18},{4,20},{6,22},{8,24},{10,26},{12,28},{14,30},{16,0},... | collective-permute-start | bytes 196616 | tf_op jit(solution)/shard_map/ppermute | solution.py:15
  206.9 4.4 %collective-permute-start.31 = (f32[128]{0:T(128)S(1)}, f32[128]{0:T(128)S(1)}, u32[]{:S(2)}, u32[]{:S(2)}) collective-permute-start(f32[128]{0:T(128)S(1)} %add.211), channel_id=1, source_target_pairs={{0,16},{2,18},{4,20},{6,22},{8,24},{10,26},{12,28},{14,30},{16,0},... | collective-permute-start | bytes 1544 | tf_op jit(solution)/shard_map/ppermute | solution.py:15
  214.2 5.0 %collective-permute-start.32 = (bf16[2,256,128]{1,2,0:T(8,128)(2,1)S(1)}, bf16[2,256,128]{1,2,0:T(8,128)(2,1)S(1)}, u32[]{:S(2)}, u32[]{:S(2)}) collective-permute-start(bf16[2,256,128]{1,2,0:T(8,128)(2,1)S(1)} %get-tuple-element.29), channel_id=1, source_target_pairs={{0,2},{2,0},{4,6},{6,4},{8,10},{10,8},{12,14},{14,12},{16,18},{18,... | collective-permute-start | bytes 393224 | tf_op jit(solution)/shard_map/ppermute | solution.py:15
  215.5 6.7 %collective-permute-start.33 = (bf16[2,256,128]{1,2,0:T(8,128)(2,1)}, bf16[2,256,128]{1,2,0:T(8,128)(2,1)}, u32[]{:S(2)}, u32[]{:S(2)}) collective-permute-start(bf16[2,256,128]{1,2,0:T(8,128)(2,1)} %get-tuple-element.32), channel_id=1, source_target_pairs={{0,4},{2,6},{4,0},{6,2},{8,12},{10,14},{12,8},{14,10},{16,20},{18,... | collective-permute-start | bytes 393224 | tf_op jit(solution)/shard_map/ppermute | solution.py:15
  216.3 9.6 %collective-permute-start.34 = (bf16[2,256,128]{1,2,0:T(8,128)(2,1)}, bf16[2,256,128]{1,2,0:T(8,128)(2,1)}, u32[]{:S(2)}, u32[]{:S(2)}) collective-permute-start(bf16[2,256,128]{1,2,0:T(8,128)(2,1)} %get-tuple-element.31), channel_id=1, source_target_pairs={{0,8},{2,10},{4,12},{6,14},{8,0},{10,2},{12,4},{14,6},{16,24},{18,... | collective-permute-start | bytes 393224 | tf_op jit(solution)/shard_map/ppermute | solution.py:15
  217.9 11.8 %collective-permute-start.35 = (bf16[2,256,128]{1,2,0:T(8,128)(2,1)}, bf16[2,256,128]{1,2,0:T(8,128)(2,1)S(1)}, u32[]{:S(2)}, u32[]{:S(2)}) collective-permute-start(bf16[2,256,128]{1,2,0:T(8,128)(2,1)} %get-tuple-element.30), channel_id=1, source_target_pairs={{0,16},{2,18},{4,20},{6,22},{8,24},{10,26},{12,28},{14,30},{16,0},... | collective-permute-start | bytes 393224 | tf_op jit(solution)/shard_map/ppermute | solution.py:15
  253.0 4.4 %collective-permute-start.39 = (f32[128]{0:T(128)S(1)}, f32[128]{0:T(128)S(1)}, u32[]{:S(2)}, u32[]{:S(2)}) collective-permute-start(f32[128]{0:T(128)S(1)} %add.217), channel_id=1, source_target_pairs={{0,16},{2,18},{4,20},{6,22},{8,24},{10,26},{12,28},{14,30},{16,0},... | collective-permute-start | bytes 1544 | tf_op jit(solution)/shard_map/ppermute | solution.py:15
  (37 other events, 401.7 us)
Sparse Core Ops, SparseCore 0:
  47.5 6.6 all-gather.4
  92.7 7.4 all-gather.6
  137.7 7.5 all-gather.8
  215.6 7.4 all-gather.10
